TPU v7x, 32 devices: a whole 2x2x4 slice. The times are simulated.
32 devices in a mesh: gx: 8 (over y, x, core), gz: 4 (over z).
Axes of the slice: x: 2, y: 2, z: 4, core: 2. Of those that a mesh axis runs over, the one named last changes fastest.
Arguments:
- heat_adjoint: float32 [128, 64, 512], P('gx', None, 'gz'), may hold values from -6 to 6
- moisture_adjoint: float32 [128, 64, 512], P('gx', None, 'gz'), may hold values from -6 to 6
- conductivity: float32 [128, 64, 512], P('gx', None, 'gz'), may hold values from 0.02 to 0.12
- labels: int32 [128, 64, 512], P('gx', None, 'gz'), may hold values from 0 to 3
- moisture_rate: float32 [4], replicated, may hold values from 0.02 to 0.1
- exchange_rates: float32 [2, 4], replicated, may hold values from 0.02 to 0.1
- checkpoints: float32 [4, 128, 64, 512], P(None, 'gx', None, 'gz'), may hold values from -6 to 6
- slot_of_step: int32 [4], replicated, may hold values from 0 to 3, each once
Outputs:
- heat_out: float32 [128, 64, 512], P('gx', None, 'gz')
- moisture_out: float32 [128, 64, 512], P('gx', None, 'gz')
- smoothed_gradient: float32 [64, 32, 256], P(None, 'gx', 'gz')
Inputs may be any that keep to these rules, and one draw needn't show every extreme that they name: slot_of_step names every slot once.
All inputs are finite; a program needn't handle non-finite values.
Results may differ from a plain program's by a relative error of at most 0.00014.
Values sent between devices are 32-bit elements; how exact they have to be, the bound alone decides.
A program may use at most 128 MiB of HBM per device.

v0:
```python
import functools

import jax
import jax.numpy as jnp
import numpy as np
from jax import lax
from jax.experimental import pallas as pl
from jax.experimental.pallas import tpu as pltpu
from jax.sharding import PartitionSpec as P

PRIOR_WEIGHT = 200.0
MESH = pl.DeviceIdType.MESH


def smoother(length):
    d = np.zeros((length, length))
    for i in range(length - 1):
        d[i, i] += 1.0
        d[i + 1, i + 1] += 1.0
        d[i, i + 1] -= 1.0
        d[i + 1, i] -= 1.0
    return np.linalg.inv(np.eye(length) + PRIOR_WEIGHT * d).astype(np.float32)


class Swap:
    def __init__(self, here, count, target, sems, index, low_face, high_face, low_halo, high_halo):
        send_sem, recv_sem = sems
        self.here, self.count = here, count
        self.faces = (low_face, high_face)
        self.halos = (low_halo, high_halo)
        self.down = pltpu.make_async_remote_copy(
            src_ref=low_face, dst_ref=high_halo,
            send_sem=send_sem.at[2 * index], recv_sem=recv_sem.at[2 * index],
            device_id=target(lax.rem(here + count - 1, count)), device_id_type=MESH)
        self.up = pltpu.make_async_remote_copy(
            src_ref=high_face, dst_ref=low_halo,
            send_sem=send_sem.at[2 * index + 1], recv_sem=recv_sem.at[2 * index + 1],
            device_id=target(lax.rem(here + 1, count)), device_id_type=MESH)

    def start(self):
        pl.when(self.here > 0)(self.down.start)
        pl.when(self.here < self.count - 1)(self.up.start)

    def recv(self):
        pl.when(self.here < self.count - 1)(self.down.wait_recv)
        pl.when(self.here > 0)(self.up.wait_recv)

    def sent(self):
        pl.when(self.here > 0)(self.down.wait_send)
        pl.when(self.here < self.count - 1)(self.up.wait_send)


def kernel(
    n_x, n_z, steps,
    heat, moist, cond, labels, rate_t, exch_t, checks, slots, minv,
    out_h, out_m, out_s,
    hm, cf, ck, lab, ra, rb, wx, wy, wzp, wzm,
    zsend_lo, zsend_hi, zlo, zhi, zcsend_lo, zcsend_hi, zclo, zchi,
    grad, hm_out, csend, crecv,
    local_sem, send_sem, recv_sem, c_send_sem, c_recv_sem,
):
    nx, ny, nz = lab.shape
    rows = ny // n_x
    gx, gz = lax.axis_index("gx"), lax.axis_index("gz")
    sems = (send_sem, recv_sem)
    to_x = lambda i: (i, gz)
    to_z = lambda i: (gx, i)
    inner = pl.ds(1, nx)

    locals_ = [
        pltpu.make_async_copy(labels, lab, local_sem.at[0]),
        pltpu.make_async_copy(heat, hm.at[0, 0, inner], local_sem.at[1]),
        pltpu.make_async_copy(moist, hm.at[0, 1, inner], local_sem.at[2]),
        pltpu.make_async_copy(cond, cf.at[0, inner], local_sem.at[3]),
        pltpu.make_async_copy(checks, ck.at[:, inner], local_sem.at[4]),
    ]
    for copy in locals_:
        copy.start()

    barrier = pltpu.get_barrier_semaphore()
    for d in range(1, n_x):
        pl.semaphore_signal(barrier, inc=1, device_id=(lax.rem(gx + d, n_x), gz), device_id_type=MESH)

    @pl.when(gz > 0)
    def _():
        pl.semaphore_signal(barrier, inc=1, device_id=(gx, gz - 1), device_id_type=MESH)

    @pl.when(gz < n_z - 1)
    def _():
        pl.semaphore_signal(barrier, inc=1, device_id=(gx, gz + 1), device_id_type=MESH)

    beside = jnp.where(gz > 0, 1, 0) + jnp.where(gz < n_z - 1, 1, 0)
    pl.semaphore_wait(barrier, n_x - 1 + beside)

    def x_swap(index, low_face, high_face, low_halo, high_halo):
        return Swap(gx, n_x, to_x, sems, index, low_face, high_face, low_halo, high_halo)

    def z_swap(index, low_face, high_face, low_halo, high_halo):
        return Swap(gz, n_z, to_z, sems, index, low_face, high_face, low_halo, high_halo)

    last = nx - 1
    x_first = [
        x_swap(0, heat.at[0], heat.at[last], hm.at[0, 0, 0], hm.at[0, 0, nx + 1]),
        x_swap(1, moist.at[0], moist.at[last], hm.at[0, 1, 0], hm.at[0, 1, nx + 1]),
        x_swap(2, cond.at[0], cond.at[last], cf.at[0, 0], cf.at[0, nx + 1]),
        x_swap(3, cf.at[1, 1], cf.at[1, nx], cf.at[1, 0], cf.at[1, nx + 1]),
    ]
    x_check = x_swap(4, checks.at[:, 0], checks.at[:, last], ck.at[:, 0], ck.at[:, nx + 1])
    z_check = z_swap(5, zcsend_lo, zcsend_hi, zclo, zchi)
    x_step = [None] + [
        x_swap(5 + t, hm.at[t, :, 1], hm.at[t, :, nx], hm.at[t, :, 0], hm.at[t, :, nx + 1])
        for t in range(1, steps)
    ]
    z_step = [
        z_swap(5 + steps + t, zsend_lo.at[t], zsend_hi.at[t], zlo.at[t], zhi.at[t])
        for t in range(steps)
    ]

    for swap in x_first[:3]:
        swap.start()

    lane = lax.broadcasted_iota(jnp.int32, (ny, nz), 1)
    row = lax.broadcasted_iota(jnp.int32, (ny, nz), 0)
    at_first, at_last = lane == 0, lane == nz - 1
    no_up = row == ny - 1

    def pick(label, table):
        return jnp.where(label == 0, table[0], jnp.where(label == 1, table[1], jnp.where(label == 2, table[2], table[3])))

    locals_[0].wait()
    table_m = [rate_t[i] for i in range(4)]
    table_a = [exch_t[0, i] for i in range(4)]
    table_b = [exch_t[1, i] for i in range(4)]

    def rates(x, carry):
        label = lab[x]
        cf[1, x + 1] = pick(label, table_m)
        ra[x] = pick(label, table_a)
        rb[x] = pick(label, table_b)
        return carry

    lax.fori_loop(0, nx, rates, 0)
    x_first[3].start()
    x_check.start()

    def pack(planes, lo_ref, hi_ref):
        def body(x, carry):
            lo, hi = carry
            for i, read in enumerate(planes):
                k = i * nx + x
                v = read(x)
                mine = lane == k
                lo = jnp.where(mine, pltpu.roll(v, k, 1), lo)
                hi = jnp.where(mine, pltpu.roll(v, k + 1, 1), hi)
            return lo, hi

        zero = jnp.zeros((ny, nz), jnp.float32)
        lo, hi = lax.fori_loop(0, nx, body, (zero, zero))
        lo_ref[...] = lo
        hi_ref[...] = hi

    for copy in locals_[1:4]:
        copy.wait()
    pack(
        [lambda x: hm[0, 0, x + 1], lambda x: hm[0, 1, x + 1], lambda x: cf[0, x + 1], lambda x: cf[1, x + 1]],
        zsend_lo.at[0], zsend_hi.at[0],
    )
    z_step[0].start()
    locals_[4].wait()
    for s in range(steps):
        pack([lambda x, s=s: ck[s, x + 1]], zcsend_lo.at[s], zcsend_hi.at[s])
    z_check.start()

    def fill(swap):
        @pl.when(swap.here == 0)
        def _():
            swap.halos[0][...] = swap.faces[0][...]

        @pl.when(swap.here == swap.count - 1)
        def _():
            swap.halos[1][...] = swap.faces[1][...]

    def fill_x(here_lo, here_hi):
        @pl.when(gx == 0)
        def _():
            here_lo[0][...] = here_lo[1][...]

        @pl.when(gx == n_x - 1)
        def _():
            here_hi[0][...] = here_hi[1][...]

    def z_low(ref, k):
        return pltpu.roll(ref, lax.rem(nz - k, nz), 1)

    def z_high(ref, k):
        return pltpu.roll(ref, nz - 1 - k, 1)

    def along_z(v, low_pack, high_pack, k):
        up = jnp.where(at_last, z_high(high_pack, k), pltpu.roll(v, nz - 1, 1))
        down = jnp.where(at_first, z_low(low_pack, k), pltpu.roll(v, 1, 1))
        return up, down

    def advance_plane(t, x):
        news = []
        olds = []
        for f in range(2):
            v = hm[t, f, x + 1]
            up, down = along_z(v, zlo[t], zhi[t], f * nx + x)
            flux = wy[f, x] * (pltpu.roll(v, ny - 1, 0) - v)
            total = (
                wx[f, x + 1] * (hm[t, f, x + 2] - v)
                + wx[f, x] * (hm[t, f, x] - v)
                + (flux - pltpu.roll(flux, 1, 0))
                + wzp[f, x] * (up - v)
                + wzm[f, x] * (down - v)
            )
            olds.append(v)
            news.append(v + total)
        trade = ra[x] * olds[0] - rb[x] * olds[1]
        return news[0] - trade, news[1] + trade

    def sense_plane(t, slot, x):
        u = ck[slot, x + 1]
        v = hm[t, 0, x + 1]
        u_up, u_down = along_z(u, zclo[slot], zchi[slot], x)
        v_up, v_down = along_z(v, zlo[t], zhi[t], x)
        across = (pltpu.roll(u, ny - 1, 0) - u) * (pltpu.roll(v, ny - 1, 0) - v)
        across = jnp.where(no_up, 0.0, across)
        return (
            (ck[slot, x + 2] - u) * (hm[t, 0, x + 2] - v)
            + (ck[slot, x] - u) * (hm[t, 0, x] - v)
            + (across + pltpu.roll(across, 1, 0))
            + (u_up - u) * (v_up - v)
            + (u_down - u) * (v_down - v)
        )

    for swap in x_first:
        swap.recv()
    z_step[0].recv()
    fill(z_step[0])
    for f in range(2):
        fill_x((hm.at[0, f, 0], hm.at[0, f, 1]), (hm.at[0, f, nx + 1], hm.at[0, f, nx]))
        fill_x((cf.at[f, 0], cf.at[f, 1]), (cf.at[f, nx + 1], cf.at[f, nx]))

    def weights(x, carry):
        for f in range(2):
            c = cf[f, x + 1]
            up, down = along_z(c, zlo[0], zhi[0], (2 + f) * nx + x)
            wx[f, x + 1] = 0.5 * (c + cf[f, x + 2])
            wy[f, x] = jnp.where(no_up, 0.0, 0.5 * (c + pltpu.roll(c, ny - 1, 0)))
            wzp[f, x] = 0.5 * (c + up)
            wzm[f, x] = 0.5 * (c + down)
        return carry

    for f in range(2):
        wx[f, 0] = 0.5 * (cf[f, 0] + cf[f, 1])
    lax.fori_loop(0, nx, weights, 0)

    for t in range(steps):
        slot = slots[t]
        if t > 0:
            x_step[t].recv()
            z_step[t].recv()
            fill(x_step[t])
            fill(z_step[t])
        if t < steps - 1:
            def put(x, carry, t=t):
                h, m = advance_plane(t, x)
                hm[t + 1, 0, x + 1] = h
                hm[t + 1, 1, x + 1] = m
                return carry

            put(0, 0)
            put(last, 0)
            x_step[t + 1].start()
            lax.fori_loop(1, last, put, 0)
            pack(
                [lambda x, t=t: hm[t + 1, 0, x + 1], lambda x, t=t: hm[t + 1, 1, x + 1]],
                zsend_lo.at[t + 1], zsend_hi.at[t + 1],
            )
            z_step[t + 1].start()
        if t == 0:
            x_check.recv()
            z_check.recv()
            fill(z_check)
            fill_x((ck.at[:, 0], ck.at[:, 1]), (ck.at[:, nx + 1], ck.at[:, nx]))
        if t < steps - 1:
            def sense(x, carry, t=t, slot=slot):
                g = sense_plane(t, slot, x)
                grad[x] = g if t == 0 else grad[x] + g
                return carry

            lax.fori_loop(0, nx, sense, 0)
        else:
            def coarsen(i, carry, t=t, slot=slot):
                total = jnp.zeros((ny, nz), jnp.float32)
                for j in range(2):
                    x = 2 * i + j
                    g = -0.5 * (grad[x] + sense_plane(t, slot, x))
                    total = total + jnp.where(lab[x] == 0, g, 0.0)
                for p in range(n_x):
                    csend[p, i] = total[p * rows : (p + 1) * rows]
                return carry

            lax.fori_loop(0, nx // 2, coarsen, 0)

    spread = []
    for d in range(1, n_x):
        peer = lax.rem(gx + d, n_x)
        copy = pltpu.make_async_remote_copy(
            src_ref=csend.at[peer], dst_ref=crecv.at[gx],
            send_sem=c_send_sem.at[d], recv_sem=c_recv_sem.at[d],
            device_id=(peer, gz), device_id_type=MESH)
        copy.start()
        spread.append(copy)
    crecv[gx] = csend[gx]

    def finish(x, carry):
        h, m = advance_plane(steps - 1, x)
        hm_out[0, x] = h
        hm_out[1, x] = m
        return carry

    lax.fori_loop(0, nx, finish, 0)
    outs = [
        pltpu.make_async_copy(hm_out.at[0], out_h, local_sem.at[5]),
        pltpu.make_async_copy(hm_out.at[1], out_m, local_sem.at[6]),
    ]
    for copy in outs:
        copy.start()

    for copy in spread:
        copy.wait_recv()
    length = n_x * (nx // 2)
    pair_row = lax.broadcasted_iota(jnp.int32, (nz, nz // 2), 0)
    pair_col = lax.broadcasted_iota(jnp.int32, (nz, nz // 2), 1)
    first = 2 * pair_col
    pairs = jnp.where((pair_row == first) | (pair_row == first + 1), 1.0, 0.0)
    for k in range(rows // 2):
        columns = (crecv[:, :, 2 * k, :] + crecv[:, :, 2 * k + 1, :]).reshape(length, nz)
        solved = jnp.dot(minv[...], columns, precision=lax.Precision.HIGHEST, preferred_element_type=jnp.float32)
        out_s[:, k, :] = jnp.dot(solved, pairs, precision=lax.Precision.HIGHEST, preferred_element_type=jnp.float32)

    for copy in spread:
        copy.wait_send()
    for swap in x_first + [x_check, z_check] + x_step[1:] + z_step:
        swap.sent()
    for copy in outs:
        copy.wait()


def on_device(n_x, n_z, heat, moist, cond, labels, rates, exchange, checks, slots):
    nx, ny, nz = heat.shape
    steps = checks.shape[0]
    half = nx // 2
    length = n_x * half
    rows = ny // n_x
    f32 = jnp.float32
    hbm = pl.BlockSpec(memory_space=pl.ANY)
    smem = pl.BlockSpec(memory_space=pltpu.SMEM)
    vmem = pl.BlockSpec(memory_space=pltpu.VMEM)
    n_swaps = 7 + 2 * steps
    scratch = [
        pltpu.VMEM((steps, 2, nx + 2, ny, nz), f32),
        pltpu.VMEM((2, nx + 2, ny, nz), f32),
        pltpu.VMEM((steps, nx + 2, ny, nz), f32),
        pltpu.VMEM((nx, ny, nz), jnp.int32),
        pltpu.VMEM((nx, ny, nz), f32),
        pltpu.VMEM((nx, ny, nz), f32),
        pltpu.VMEM((2, nx + 1, ny, nz), f32),
        pltpu.VMEM((2, nx, ny, nz), f32),
        pltpu.VMEM((2, nx, ny, nz), f32),
        pltpu.VMEM((2, nx, ny, nz), f32),
    ] + [pltpu.VMEM((steps, ny, nz), f32) for _ in range(8)] + [
        pltpu.VMEM((nx, ny, nz), f32),
        pltpu.VMEM((2, nx, ny, nz), f32),
        pltpu.VMEM((n_x, half, rows, nz), f32),
        pltpu.VMEM((n_x, half, rows, nz), f32),
        pltpu.SemaphoreType.DMA((7,)),
        pltpu.SemaphoreType.DMA((2 * n_swaps,)),
        pltpu.SemaphoreType.DMA((2 * n_swaps,)),
        pltpu.SemaphoreType.DMA((n_x,)),
        pltpu.SemaphoreType.DMA((n_x,)),
    ]
    return pl.pallas_call(
        functools.partial(kernel, n_x, n_z, steps),
        out_shape=(
            jax.ShapeDtypeStruct(heat.shape, f32),
            jax.ShapeDtypeStruct(heat.shape, f32),
            jax.ShapeDtypeStruct((length, rows // 2, nz // 2), f32),
        ),
        in_specs=[hbm, hbm, hbm, hbm, smem, smem, hbm, smem, vmem],
        out_specs=(hbm, hbm, vmem),
        scratch_shapes=scratch,
        compiler_params=pltpu.CompilerParams(
            collective_id=0, has_side_effects=True, vmem_limit_bytes=48 * 1024 * 1024
        ),
        name="adjoint_window",
    )(heat, moist, cond, labels, rates, exchange, checks, slots, jnp.asarray(smoother(length)))


def solution(mesh):
    grid = P("gx", None, "gz")
    in_specs = (grid, grid, grid, grid, P(), P(), P(None, "gx", None, "gz"), P())
    out_specs = (grid, grid, P(None, "gx", "gz"))
    return jax.shard_map(
        functools.partial(on_device, mesh.shape["gx"], mesh.shape["gz"]),
        mesh=mesh, in_specs=in_specs, out_specs=out_specs, check_vma=False,
    )
```

profile of v0, /device:TPU:0, one launch (start us, length us, event | category | flops | bytes accessed | tf_op | source)
XLA Modules:
  0.0 54.6 jit_solution(11001763768359782949)
XLA Ops:
  0.6 0.0 copy-start
  0.6 1.6 %copy-done = f32[4,16,64,128]{3,2,1,0:T(8,128)S(1)} copy-done((f32[4,16,64,128]{3,2,1,0:T(8,128)S(1)}, f32[4,16,64,128]{3,2,1,0:T(8,128)}, u32[]{:S(2)}) %copy-start) | copy-done | bytes 2097176
  2.2 0.0 copy-start.1
  2.2 1.0 %copy-done.1 = f32[16,64,128]{2,1,0:T(8,128)S(1)} copy-done((f32[16,64,128]{2,1,0:T(8,128)S(1)}, f32[16,64,128]{2,1,0:T(8,128)}, u32[]{:S(2)}) %copy-start.1) | copy-done | bytes 524312
  3.3 0.0 copy-start.2
  3.3 1.0 %copy-done.2 = f32[16,64,128]{2,1,0:T(8,128)S(1)} copy-done((f32[16,64,128]{2,1,0:T(8,128)S(1)}, f32[16,64,128]{2,1,0:T(8,128)}, u32[]{:S(2)}) %copy-start.2) | copy-done | bytes 524312
  4.3 0.0 copy-start.3
  4.3 1.0 %copy-done.3 = f32[16,64,128]{2,1,0:T(8,128)S(1)} copy-done((f32[16,64,128]{2,1,0:T(8,128)S(1)}, f32[16,64,128]{2,1,0:T(8,128)}, u32[]{:S(2)}) %copy-start.3) | copy-done | bytes 524312
  5.4 0.0 copy-start.4
  5.4 1.0 %copy-done.4 = s32[16,64,128]{2,1,0:T(8,128)S(1)} copy-done((s32[16,64,128]{2,1,0:T(8,128)S(1)}, s32[16,64,128]{2,1,0:T(8,128)}, u32[]{:S(2)}) %copy-start.4) | copy-done | bytes 524312
  6.4 0.0 copy-start.5
  6.4 0.8 %copy-done.5 = f32[64,64]{1,0:T(8,128)S(1)} copy-done((f32[64,64]{1,0:T(8,128)S(1)}, f32[64,64]{1,0:T(8,128)}, u32[]{:S(2)}) %copy-start.5) | copy-done | bytes 16408
  7.2 0.0 copy-start.6
  7.2 0.7 %copy-done.6 = f32[2,4]{1,0:T(2,128)S(1)} copy-done((f32[2,4]{1,0:T(2,128)S(1)}, f32[2,4]{1,0:T(2,128)}, u32[]{:S(2)}) %copy-start.6) | copy-done | bytes 56
  7.8 0.0 copy-start.7
  7.8 0.7 %copy-done.7 = f32[4]{0:T(128)S(1)} copy-done((f32[4]{0:T(128)S(1)}, f32[4]{0:T(128)}, u32[]{:S(2)}) %copy-start.7) | copy-done | bytes 40
  8.5 0.0 copy-start.8
  8.5 0.7 %copy-done.8 = s32[4]{0:T(128)S(1)} copy-done((s32[4]{0:T(128)S(1)}, s32[4]{0:T(128)}, u32[]{:S(2)}) %copy-start.8) | copy-done | bytes 40
  9.1 43.2 %adjoint_window.1 = (f32[16,64,128]{2,1,0:T(8,128)S(1)}, f32[16,64,128]{2,1,0:T(8,128)S(1)}, f32[64,4,64]{2,1,0:T(4,128)S(1)}) custom-call(f32[16,64,128]{2,1,0:T(8,128)S(1)} %copy-done.1, f32[16,64,128]{2,1,0:T(8,128)S(1)} %copy-done.2, f32[16,64,128]{2,1,0:T(8,128)S(1)} %copy-done.3, s32[16,64,128]{2,1,0:T(8,128)S(1)} %copy-done.4, f32[4]{0:T(128)S(1)} %copy-done.7, ...), custom_call_target="tpu_custom_call" | custom-call | tf_op jit(solution)/shard_map/adjoint_window/pallas_call | solution.py:385
  52.3 0.8 %copy.15 = f32[16,64,128]{2,1,0:T(8,128)} copy(f32[16,64,128]{2,1,0:T(8,128)S(1)} %get-tuple-element.6) | data formatting | bytes 1048576
  53.1 0.8 %copy.16 = f32[16,64,128]{2,1,0:T(8,128)} copy(f32[16,64,128]{2,1,0:T(8,128)S(1)} %get-tuple-element.7) | data formatting | bytes 1048576
  53.9 0.7 %copy.17 = f32[64,4,64]{2,1,0:T(4,128)} copy(f32[64,4,64]{2,1,0:T(4,128)S(1)} %get-tuple-element.8) | data formatting | bytes 131072
Async XLA Ops:
  0.6 1.6 %copy-start = (f32[4,16,64,128]{3,2,1,0:T(8,128)S(1)}, f32[4,16,64,128]{3,2,1,0:T(8,128)}, u32[]{:S(2)}) copy-start(f32[4,16,64,128]{3,2,1,0:T(8,128)} %checks.1) | copy-start | bytes 6291460
  2.2 1.0 %copy-start.1 = (f32[16,64,128]{2,1,0:T(8,128)S(1)}, f32[16,64,128]{2,1,0:T(8,128)}, u32[]{:S(2)}) copy-start(f32[16,64,128]{2,1,0:T(8,128)} %heat.1) | copy-start | bytes 1572868
  3.3 1.0 %copy-start.2 = (f32[16,64,128]{2,1,0:T(8,128)S(1)}, f32[16,64,128]{2,1,0:T(8,128)}, u32[]{:S(2)}) copy-start(f32[16,64,128]{2,1,0:T(8,128)} %moist.1) | copy-start | bytes 1572868
  4.3 1.0 %copy-start.3 = (f32[16,64,128]{2,1,0:T(8,128)S(1)}, f32[16,64,128]{2,1,0:T(8,128)}, u32[]{:S(2)}) copy-start(f32[16,64,128]{2,1,0:T(8,128)} %cond.1) | copy-start | bytes 1572868
  5.4 1.0 %copy-start.4 = (s32[16,64,128]{2,1,0:T(8,128)S(1)}, s32[16,64,128]{2,1,0:T(8,128)}, u32[]{:S(2)}) copy-start(s32[16,64,128]{2,1,0:T(8,128)} %labels.1) | copy-start | bytes 1572868
  6.4 0.8 %copy-start.5 = (f32[64,64]{1,0:T(8,128)S(1)}, f32[64,64]{1,0:T(8,128)}, u32[]{:S(2)}) copy-start(f32[64,64]{1,0:T(8,128)} %constant.2.clone.minv) | copy-start | bytes 49156
  7.2 0.7 %copy-start.6 = (f32[2,4]{1,0:T(2,128)S(1)}, f32[2,4]{1,0:T(2,128)}, u32[]{:S(2)}) copy-start(f32[2,4]{1,0:T(2,128)} %exch_t.1) | copy-start | bytes 100
  7.8 0.7 %copy-start.7 = (f32[4]{0:T(128)S(1)}, f32[4]{0:T(128)}, u32[]{:S(2)}) copy-start(f32[4]{0:T(128)} %rate_t.1) | copy-start | bytes 52
  8.5 0.7 %copy-start.8 = (s32[4]{0:T(128)S(1)}, s32[4]{0:T(128)}, u32[]{:S(2)}) copy-start(s32[4]{0:T(128)} %slots.1) | copy-start | bytes 52
where the time goes:
time: 55 us; the launch traced here: 54.6 us
  Pallas kernels  43.2 us (79%)
  local copies, waits for them, and re-layouts  10.7 us (19%)
  between operations  0.66 us (1%)
    pallas_call x1, Pallas kernels, on_device(): pl.pallas_call(functools.partial(kernel, n_x, n_z, steps), out_shape=(jax...  43.2 us
    unnamed x21, local copies, waits for them, and re-layouts  10.7 us

commit v1 on v0

--- a/solution.py
+++ b/solution.py
@@ -10,6 +10,7 @@
 
 PRIOR_WEIGHT = 200.0
 MESH = pl.DeviceIdType.MESH
+TOGETHER = 4
 
 
 def smoother(length):
@@ -55,7 +56,7 @@
     heat, moist, cond, labels, rate_t, exch_t, checks, slots, minv,
     out_h, out_m, out_s,
     hm, cf, ck, lab, ra, rb, wx, wy, wzp, wzm,
-    zsend_lo, zsend_hi, zlo, zhi, zcsend_lo, zcsend_hi, zclo, zchi,
+    zsend, zlo, zhi, zhalo, zcsend, zclo, zchi, zchalo,
     grad, hm_out, csend, crecv,
     local_sem, send_sem, recv_sem, c_send_sem, c_recv_sem,
 ):
@@ -63,6 +64,17 @@
     rows = ny // n_x
     gx, gz = lax.axis_index("gx"), lax.axis_index("gz")
     sems = (send_sem, recv_sem)
+
+    def over(low, high, body):
+        def block(i, carry):
+            for j in range(TOGETHER):
+                body(low + i * TOGETHER + j)
+            return carry
+
+        lax.fori_loop(0, (high - low) // TOGETHER, block, 0)
+        for x in range(low + (high - low) // TOGETHER * TOGETHER, high):
+            body(x)
+
     to_x = lambda i: (i, gz)
     to_z = lambda i: (gx, i)
     inner = pl.ds(1, nx)
@@ -106,13 +118,13 @@
         x_swap(3, cf.at[1, 1], cf.at[1, nx], cf.at[1, 0], cf.at[1, nx + 1]),
     ]
     x_check = x_swap(4, checks.at[:, 0], checks.at[:, last], ck.at[:, 0], ck.at[:, nx + 1])
-    z_check = z_swap(5, zcsend_lo, zcsend_hi, zclo, zchi)
+    z_check = z_swap(5, zcsend, zcsend, zclo, zchi)
     x_step = [None] + [
         x_swap(5 + t, hm.at[t, :, 1], hm.at[t, :, nx], hm.at[t, :, 0], hm.at[t, :, nx + 1])
         for t in range(1, steps)
     ]
     z_step = [
-        z_swap(5 + steps + t, zsend_lo.at[t], zsend_hi.at[t], zlo.at[t], zhi.at[t])
+        z_swap(5 + steps + t, zsend.at[t], zsend.at[t], zlo.at[t], zhi.at[t])
         for t in range(steps)
     ]
 
@@ -123,6 +135,8 @@
     row = lax.broadcasted_iota(jnp.int32, (ny, nz), 0)
     at_first, at_last = lane == 0, lane == nz - 1
     no_up = row == ny - 1
+    pair = lax.shift_right_logical(lane, 1)
+    even = lax.rem(lane, 2) == 0
 
     def pick(label, table):
         return jnp.where(label == 0, table[0], jnp.where(label == 1, table[1], jnp.where(label == 2, table[2], table[3])))
@@ -132,43 +146,40 @@
     table_a = [exch_t[0, i] for i in range(4)]
     table_b = [exch_t[1, i] for i in range(4)]
 
-    def rates(x, carry):
+    def rates(x):
         label = lab[x]
         cf[1, x + 1] = pick(label, table_m)
         ra[x] = pick(label, table_a)
         rb[x] = pick(label, table_b)
-        return carry
-
-    lax.fori_loop(0, nx, rates, 0)
+
+    over(0, nx, rates)
     x_first[3].start()
     x_check.start()
 
-    def pack(planes, lo_ref, hi_ref):
-        def body(x, carry):
-            lo, hi = carry
-            for i, read in enumerate(planes):
-                k = i * nx + x
-                v = read(x)
-                mine = lane == k
-                lo = jnp.where(mine, pltpu.roll(v, k, 1), lo)
-                hi = jnp.where(mine, pltpu.roll(v, k + 1, 1), hi)
-            return lo, hi
-
-        zero = jnp.zeros((ny, nz), jnp.float32)
-        lo, hi = lax.fori_loop(0, nx, body, (zero, zero))
-        lo_ref[...] = lo
-        hi_ref[...] = hi
+    def pack(planes, ref):
+        total = jnp.zeros((ny, nz), jnp.float32)
+        for j, v in enumerate(planes):
+            total = jnp.where(pair == j, pltpu.roll(v, (2 * j + 1) % nz, 1), total)
+        ref[...] = total
+
+    def merge(own, low_pack, high_pack, ref):
+        ref[...] = own[...]
+
+        @pl.when(gz > 0)
+        def _():
+            ref[...] = jnp.where(even, ref[...], pltpu.roll(low_pack[...], 1, 1))
+
+        @pl.when(gz < n_z - 1)
+        def _():
+            ref[...] = jnp.where(even, pltpu.roll(high_pack[...], nz - 1, 1), ref[...])
 
     for copy in locals_[1:4]:
         copy.wait()
-    pack(
-        [lambda x: hm[0, 0, x + 1], lambda x: hm[0, 1, x + 1], lambda x: cf[0, x + 1], lambda x: cf[1, x + 1]],
-        zsend_lo.at[0], zsend_hi.at[0],
-    )
+    pack([src[i, x + 1] for src in (hm.at[0], cf) for i in range(2) for x in range(nx)], zsend.at[0])
     z_step[0].start()
     locals_[4].wait()
     for s in range(steps):
-        pack([lambda x, s=s: ck[s, x + 1]], zcsend_lo.at[s], zcsend_hi.at[s])
+        pack([ck[s, x + 1] for x in range(nx)], zcsend.at[s])
     z_check.start()
 
     def fill(swap):
@@ -189,15 +200,10 @@
         def _():
             here_hi[0][...] = here_hi[1][...]
 
-    def z_low(ref, k):
-        return pltpu.roll(ref, lax.rem(nz - k, nz), 1)
-
-    def z_high(ref, k):
-        return pltpu.roll(ref, nz - 1 - k, 1)
-
-    def along_z(v, low_pack, high_pack, k):
-        up = jnp.where(at_last, z_high(high_pack, k), pltpu.roll(v, nz - 1, 1))
-        down = jnp.where(at_first, z_low(low_pack, k), pltpu.roll(v, 1, 1))
+    def along_z(v, halo, j):
+        ends = pltpu.roll(halo, nz - 1 - 2 * j, 1)
+        up = jnp.where(at_last, ends, pltpu.roll(v, nz - 1, 1))
+        down = jnp.where(at_first, ends, pltpu.roll(v, 1, 1))
         return up, down
 
     def advance_plane(t, x):
@@ -205,7 +211,7 @@
         olds = []
         for f in range(2):
             v = hm[t, f, x + 1]
-            up, down = along_z(v, zlo[t], zhi[t], f * nx + x)
+            up, down = along_z(v, zhalo[t], f * nx + x)
             flux = wy[f, x] * (pltpu.roll(v, ny - 1, 0) - v)
             total = (
                 wx[f, x + 1] * (hm[t, f, x + 2] - v)
@@ -222,8 +228,8 @@
     def sense_plane(t, slot, x):
         u = ck[slot, x + 1]
         v = hm[t, 0, x + 1]
-        u_up, u_down = along_z(u, zclo[slot], zchi[slot], x)
-        v_up, v_down = along_z(v, zlo[t], zhi[t], x)
+        u_up, u_down = along_z(u, zchalo[slot], x)
+        v_up, v_down = along_z(v, zhalo[t], x)
         across = (pltpu.roll(u, ny - 1, 0) - u) * (pltpu.roll(v, ny - 1, 0) - v)
         across = jnp.where(no_up, 0.0, across)
         return (
@@ -237,24 +243,23 @@
     for swap in x_first:
         swap.recv()
     z_step[0].recv()
-    fill(z_step[0])
+    merge(zsend.at[0], zlo.at[0], zhi.at[0], zhalo.at[0])
     for f in range(2):
         fill_x((hm.at[0, f, 0], hm.at[0, f, 1]), (hm.at[0, f, nx + 1], hm.at[0, f, nx]))
         fill_x((cf.at[f, 0], cf.at[f, 1]), (cf.at[f, nx + 1], cf.at[f, nx]))
 
-    def weights(x, carry):
+    def weights(x):
         for f in range(2):
             c = cf[f, x + 1]
-            up, down = along_z(c, zlo[0], zhi[0], (2 + f) * nx + x)
+            up, down = along_z(c, zhalo[0], (2 + f) * nx + x)
             wx[f, x + 1] = 0.5 * (c + cf[f, x + 2])
             wy[f, x] = jnp.where(no_up, 0.0, 0.5 * (c + pltpu.roll(c, ny - 1, 0)))
             wzp[f, x] = 0.5 * (c + up)
             wzm[f, x] = 0.5 * (c + down)
-        return carry
 
     for f in range(2):
         wx[f, 0] = 0.5 * (cf[f, 0] + cf[f, 1])
-    lax.fori_loop(0, nx, weights, 0)
+    over(0, nx, weights)
 
     for t in range(steps):
         slot = slots[t]
@@ -262,35 +267,31 @@
             x_step[t].recv()
             z_step[t].recv()
             fill(x_step[t])
-            fill(z_step[t])
+            merge(zsend.at[t], zlo.at[t], zhi.at[t], zhalo.at[t])
         if t < steps - 1:
-            def put(x, carry, t=t):
+            def put(x, t=t):
                 h, m = advance_plane(t, x)
                 hm[t + 1, 0, x + 1] = h
                 hm[t + 1, 1, x + 1] = m
-                return carry
-
-            put(0, 0)
-            put(last, 0)
+
+            put(0)
+            put(last)
             x_step[t + 1].start()
-            lax.fori_loop(1, last, put, 0)
-            pack(
-                [lambda x, t=t: hm[t + 1, 0, x + 1], lambda x, t=t: hm[t + 1, 1, x + 1]],
-                zsend_lo.at[t + 1], zsend_hi.at[t + 1],
-            )
+            over(1, last, put)
+            pack([hm[t + 1, f, x + 1] for f in range(2) for x in range(nx)], zsend.at[t + 1])
             z_step[t + 1].start()
         if t == 0:
             x_check.recv()
             z_check.recv()
-            fill(z_check)
+            for s in range(steps):
+                merge(zcsend.at[s], zclo.at[s], zchi.at[s], zchalo.at[s])
             fill_x((ck.at[:, 0], ck.at[:, 1]), (ck.at[:, nx + 1], ck.at[:, nx]))
         if t < steps - 1:
-            def sense(x, carry, t=t, slot=slot):
+            def sense(x, t=t, slot=slot):
                 g = sense_plane(t, slot, x)
                 grad[x] = g if t == 0 else grad[x] + g
-                return carry
-
-            lax.fori_loop(0, nx, sense, 0)
+
+            over(0, nx, sense)
         else:
             def coarsen(i, carry, t=t, slot=slot):
                 total = jnp.zeros((ny, nz), jnp.float32)
@@ -315,13 +316,12 @@
         spread.append(copy)
     crecv[gx] = csend[gx]
 
-    def finish(x, carry):
+    def finish(x):
         h, m = advance_plane(steps - 1, x)
         hm_out[0, x] = h
         hm_out[1, x] = m
-        return carry
-
-    lax.fori_loop(0, nx, finish, 0)
+
+    over(0, nx, finish)
     outs = [
         pltpu.make_async_copy(hm_out.at[0], out_h, local_sem.at[5]),
         pltpu.make_async_copy(hm_out.at[1], out_m, local_sem.at[6]),
@@ -336,10 +336,16 @@
     pair_col = lax.broadcasted_iota(jnp.int32, (nz, nz // 2), 1)
     first = 2 * pair_col
     pairs = jnp.where((pair_row == first) | (pair_row == first + 1), 1.0, 0.0)
+    columns = [
+        (crecv[:, :, 2 * k, :] + crecv[:, :, 2 * k + 1, :]).reshape(length, nz) for k in range(rows // 2)
+    ]
+    exact = dict(precision=lax.Precision.HIGHEST, preferred_element_type=jnp.float32)
+    solved = jnp.dot(minv[...], jnp.concatenate(columns, axis=1), **exact)
+    halves = jnp.dot(
+        jnp.concatenate([solved[:, k * nz : (k + 1) * nz] for k in range(rows // 2)], axis=0), pairs, **exact
+    )
     for k in range(rows // 2):
-        columns = (crecv[:, :, 2 * k, :] + crecv[:, :, 2 * k + 1, :]).reshape(length, nz)
-        solved = jnp.dot(minv[...], columns, precision=lax.Precision.HIGHEST, preferred_element_type=jnp.float32)
-        out_s[:, k, :] = jnp.dot(solved, pairs, precision=lax.Precision.HIGHEST, preferred_element_type=jnp.float32)
+        out_s[:, k, :] = halves[k * length : (k + 1) * length]
 
     for copy in spread:
         copy.wait_send()
@@ -393,7 +399,7 @@
         out_specs=(hbm, hbm, vmem),
         scratch_shapes=scratch,
         compiler_params=pltpu.CompilerParams(
-            collective_id=0, has_side_effects=True, vmem_limit_bytes=48 * 1024 * 1024
+            collective_id=0, has_side_effects=True, vmem_limit_bytes=62 * 1024 * 1024
         ),
         name="adjoint_window",
     )(heat, moist, cond, labels, rates, exchange, checks, slots, jnp.asarray(smoother(length)))

time: 55 us -> 38.2 us (0.69)
  Pallas kernels: 43.2 us -> 32.9 us
  local copies, waits for them, and re-layouts: 10.7 us -> 4.46 us
    pallas_call x1, Pallas kernels: 43.2 us -> 32.9 us  [on_device(): pl.pallas_call(functools.partial(kernel, n_x, n_z, steps), out_shape=(jax...]
    unnamed x21 -> x5, local copies, waits for them, and re-layouts: 10.7 us -> 4.46 us
where the time goes in v1:
time: 38.2 us; the launch traced here: 38 us
  Pallas kernels  32.9 us (86%)
  local copies, waits for them, and re-layouts  4.46 us (12%)
  between operations  0.65 us (2%)
    pallas_call x1, Pallas kernels, on_device(): pl.pallas_call(functools.partial(kernel, n_x, n_z, steps), out_shape=(jax...  32.9 us
    unnamed x5, local copies, waits for them, and re-layouts  4.46 us

profile of v1, /device:TPU:0, one launch (start us, length us, event | category | flops | bytes accessed | tf_op | source)
XLA Modules:
  0.0 38.0 jit_solution(2593389237737798368)
XLA Ops:
  0.6 32.9 %adjoint_window.1 = (f32[16,64,128]{2,1,0:T(8,128)}, f32[16,64,128]{2,1,0:T(8,128)}, f32[64,4,64]{2,1,0:T(4,128)}) custom-call(f32[16,64,128]{2,1,0:T(8,128)} %heat.1, f32[16,64,128]{2,1,0:T(8,128)} %moist.1, f32[16,64,128]{2,1,0:T(8,128)} %cond.1, s32[16,64,128]{2,1,0:T(8,128)} %labels.1, f32[4]{0:T(128)} %rate_t.1, f32[2,4]{1,0:T(2,128)} %exch_t.1, ...), custom_call_target="tpu_custom_call" | custom-call | tf_op jit(solution)/shard_map/adjoint_window/pallas_call | solution.py:391
  33.5 0.0 copy-start
  33.5 1.9 %copy.15 = f32[16,64,128]{2,1,0:T(8,128)} copy(f32[16,64,128]{2,1,0:T(8,128)} %get-tuple-element.6) | data formatting | bytes 1048576
  35.4 1.9 %copy.16 = f32[16,64,128]{2,1,0:T(8,128)} copy(f32[16,64,128]{2,1,0:T(8,128)} %get-tuple-element.7) | data formatting | bytes 1048576
  37.3 0.0 copy-done
  37.3 0.7 %copy.17 = f32[64,4,64]{2,1,0:T(4,128)} copy(f32[64,4,64]{2,1,0:T(4,128)S(1)} %copy-done) | data formatting | bytes 131072
Async XLA Ops:
  33.5 3.8 %copy-start = (f32[64,4,64]{2,1,0:T(4,128)S(1)}, f32[64,4,64]{2,1,0:T(4,128)}, u32[]{:S(2)}) copy-start(f32[64,4,64]{2,1,0:T(4,128)} %get-tuple-element.8) | copy-start | bytes 196612

commit v2 on v1

--- a/solution.py
+++ b/solution.py
@@ -101,9 +101,6 @@
     def _():
         pl.semaphore_signal(barrier, inc=1, device_id=(gx, gz + 1), device_id_type=MESH)
 
-    beside = jnp.where(gz > 0, 1, 0) + jnp.where(gz < n_z - 1, 1, 0)
-    pl.semaphore_wait(barrier, n_x - 1 + beside)
-
     def x_swap(index, low_face, high_face, low_halo, high_halo):
         return Swap(gx, n_x, to_x, sems, index, low_face, high_face, low_halo, high_halo)
 
@@ -128,9 +125,6 @@
         for t in range(steps)
     ]
 
-    for swap in x_first[:3]:
-        swap.start()
-
     lane = lax.broadcasted_iota(jnp.int32, (ny, nz), 1)
     row = lax.broadcasted_iota(jnp.int32, (ny, nz), 0)
     at_first, at_last = lane == 0, lane == nz - 1
@@ -153,8 +147,6 @@
         rb[x] = pick(label, table_b)
 
     over(0, nx, rates)
-    x_first[3].start()
-    x_check.start()
 
     def pack(planes, ref):
         total = jnp.zeros((ny, nz), jnp.float32)
@@ -176,7 +168,12 @@
     for copy in locals_[1:4]:
         copy.wait()
     pack([src[i, x + 1] for src in (hm.at[0], cf) for i in range(2) for x in range(nx)], zsend.at[0])
+    beside = jnp.where(gz > 0, 1, 0) + jnp.where(gz < n_z - 1, 1, 0)
+    pl.semaphore_wait(barrier, n_x - 1 + beside)
     z_step[0].start()
+    for swap in x_first:
+        swap.start()
+    x_check.start()
     locals_[4].wait()
     for s in range(steps):
         pack([ck[s, x + 1] for x in range(nx)], zcsend.at[s])
@@ -353,6 +350,11 @@
         swap.sent()
     for copy in outs:
         copy.wait()
+
+
+def hand_on(*refs):
+    for i in range(3):
+        refs[3 + i][...] = refs[i][...]
 
 
 def on_device(n_x, n_z, heat, moist, cond, labels, rates, exchange, checks, slots):
@@ -388,7 +390,7 @@
         pltpu.SemaphoreType.DMA((n_x,)),
         pltpu.SemaphoreType.DMA((n_x,)),
     ]
-    return pl.pallas_call(
+    done = pl.pallas_call(
         functools.partial(kernel, n_x, n_z, steps),
         out_shape=(
             jax.ShapeDtypeStruct(heat.shape, f32),
@@ -403,6 +405,14 @@
         ),
         name="adjoint_window",
     )(heat, moist, cond, labels, rates, exchange, checks, slots, jnp.asarray(smoother(length)))
+    return pl.pallas_call(
+        hand_on,
+        out_shape=tuple(jax.ShapeDtypeStruct(a.shape, a.dtype) for a in done),
+        in_specs=[vmem] * 3,
+        out_specs=(vmem,) * 3,
+        compiler_params=pltpu.CompilerParams(vmem_limit_bytes=62 * 1024 * 1024),
+        name="hand_on",
+    )(*done)
 
 
 def solution(mesh):

time: 38.2 us -> 36 us (0.942)
  local copies, waits for them, and re-layouts: 4.46 us -> 0 us
  Pallas kernels: 32.9 us -> 35.1 us
    unnamed x5 -> x0, local copies, waits for them, and re-layouts: 4.46 us -> none
    pallas_call x0 -> x1, Pallas kernels: none -> 2.26 us  [on_device(): pl.pallas_call(hand_on, out_shape=tuple((jax.ShapeDtypeStruct(a.shape, a....]
where the time goes in v2:
time: 36 us; the launch traced here: 35.8 us
  Pallas kernels  35.1 us (98%)
  between operations  0.64 us (2%)
    pallas_call x1, Pallas kernels, on_device(): pl.pallas_call(functools.partial(kernel, n_x, n_z, steps), out_shape=(jax...  32.9 us
    pallas_call x1, Pallas kernels, on_device(): pl.pallas_call(hand_on, out_shape=tuple((jax.ShapeDtypeStruct(a.shape, a....  2.26 us

profile of v2, /device:TPU:0, one launch (start us, length us, event | category | flops | bytes accessed | tf_op | source)
XLA Modules:
  0.0 35.8 jit_solution(3734148941845698846)
XLA Ops:
  0.6 32.9 %adjoint_window.1 = (f32[16,64,128]{2,1,0:T(8,128)}, f32[16,64,128]{2,1,0:T(8,128)}, f32[64,4,64]{2,1,0:T(4,128)}) custom-call(f32[16,64,128]{2,1,0:T(8,128)} %heat.1, f32[16,64,128]{2,1,0:T(8,128)} %moist.1, f32[16,64,128]{2,1,0:T(8,128)} %cond.1, s32[16,64,128]{2,1,0:T(8,128)} %labels.1, f32[4]{0:T(128)} %rate_t.1, f32[2,4]{1,0:T(2,128)} %exch_t.1, ...), custom_call_target="tpu_custom_call" | custom-call | tf_op jit(solution)/shard_map/adjoint_window/pallas_call | solution.py:393
  33.5 2.3 %hand_on.1 = (f32[16,64,128]{2,1,0:T(8,128)}, f32[16,64,128]{2,1,0:T(8,128)}, f32[64,4,64]{2,1,0:T(4,128)}) custom-call(f32[16,64,128]{2,1,0:T(8,128)} %get-tuple-element.6.refs_0_, f32[16,64,128]{2,1,0:T(8,128)} %get-tuple-element.7.refs_1_, f32[64,4,64]{2,1,0:T(4,128)} %get-tuple-element.8.refs_2_), custom_call_target="tpu_custom_call" | custom-call | tf_op jit(solution)/shard_map/hand_on/pallas_call | solution.py:408

commit v3 on v2

--- a/solution.py
+++ b/solution.py
@@ -10,7 +10,7 @@
 
 PRIOR_WEIGHT = 200.0
 MESH = pl.DeviceIdType.MESH
-TOGETHER = 4
+TOGETHER = 8
 
 
 def smoother(length):

time: 36 us -> 35.2 us (0.978)
  Pallas kernels: 35.1 us -> 34.3 us
    pallas_call x1, Pallas kernels: 32.9 us -> 32.1 us  [on_device(): pl.pallas_call(functools.partial(kernel, n_x, n_z, steps), out_shape=(jax...]
where the time goes in v3:
time: 35.2 us; the launch traced here: 35 us
  Pallas kernels  34.3 us (97%)
  between operations  0.64 us (2%)
    pallas_call x1, Pallas kernels, on_device(): pl.pallas_call(functools.partial(kernel, n_x, n_z, steps), out_shape=(jax...  32.1 us
    pallas_call x1, Pallas kernels, on_device(): pl.pallas_call(hand_on, out_shape=tuple((jax.ShapeDtypeStruct(a.shape, a....  2.26 us

profile of v3, /device:TPU:0, one launch (start us, length us, event | category | flops | bytes accessed | tf_op | source)
XLA Modules:
  0.0 35.0 jit_solution(10465503087283565908)
XLA Ops:
  0.6 32.1 %adjoint_window.1 = (f32[16,64,128]{2,1,0:T(8,128)}, f32[16,64,128]{2,1,0:T(8,128)}, f32[64,4,64]{2,1,0:T(4,128)}) custom-call(f32[16,64,128]{2,1,0:T(8,128)} %heat.1, f32[16,64,128]{2,1,0:T(8,128)} %moist.1, f32[16,64,128]{2,1,0:T(8,128)} %cond.1, s32[16,64,128]{2,1,0:T(8,128)} %labels.1, f32[4]{0:T(128)} %rate_t.1, f32[2,4]{1,0:T(2,128)} %exch_t.1, ...), custom_call_target="tpu_custom_call" | custom-call | tf_op jit(solution)/shard_map/adjoint_window/pallas_call | solution.py:393
  32.7 2.3 %hand_on.1 = (f32[16,64,128]{2,1,0:T(8,128)}, f32[16,64,128]{2,1,0:T(8,128)}, f32[64,4,64]{2,1,0:T(4,128)}) custom-call(f32[16,64,128]{2,1,0:T(8,128)} %get-tuple-element.6.refs_0_, f32[16,64,128]{2,1,0:T(8,128)} %get-tuple-element.7.refs_1_, f32[64,4,64]{2,1,0:T(4,128)} %get-tuple-element.8.refs_2_), custom_call_target="tpu_custom_call" | custom-call | tf_op jit(solution)/shard_map/hand_on/pallas_call | solution.py:408
